TPU v7x, 32 devices: a whole 2x2x4 slice. The times are simulated.
32 devices in a mesh: groups: 2 (over x), dp: 2 (over core), tensor: 8 (over z, y).
Axes of the slice: x: 2, y: 2, z: 4, core: 2. Of those that a mesh axis runs over, the one named last changes fastest.
Arguments:
- gate_preactivation: bfloat16 [3072, 16384], P(('groups', 'dp'), 'tensor'), parts along dimension 0, may hold values from -6 to 6
- up_preactivation: bfloat16 [3072, 16384], P(('groups', 'dp'), 'tensor'), parts along dimension 0, may hold values from -6 to 6
- down_matrix: bfloat16 [16384, 8192], P('tensor'), may hold values from -0.0625 to 0.0625
- adapter_input_maps: bfloat16 [16, 64, 16384], P(('dp', 'tensor')), may hold values from -0.046875 to 0.046875
- adapter_output_maps: bfloat16 [16, 64, 8192], P(('dp', 'tensor')), may hold values from -0.75 to 0.75
- row_adapter_index: int32 [3072], P(('groups', 'dp')), parts along dimension 0, may hold values from 0 to 15
- adapter_storage_slot: int32 [16], replicated, may hold values from 0 to 15, each once
Outputs:
- mixed: bfloat16 [3072, 8192], P(('groups', 'dp'), 'tensor'), parts along dimension 0
There are 2 independent parts, one for each index of `groups`. A program takes and returns all parts, laid end to end along the dimension named above; an argument that names none is the same for every part. Nothing has to cross between parts.
Inputs may be any that keep to these rules, and one draw needn't show every extreme that they name: `adapter_storage_slot`: each slot belongs to exactly one adapter.
All inputs are finite; a program needn't handle non-finite values.
Results may differ from a plain program's by a relative error of at most 0.014.
Values may be sent and summed in bfloat16 or wider, within the bound.
A program may use at most 192 MiB of HBM per device.

v0:
```python
import jax
import jax.numpy as jnp
from jax import lax
from jax.sharding import PartitionSpec as P


def local(
    gate_preactivation,
    up_preactivation,
    down_matrix,
    adapter_input_maps,
    adapter_output_maps,
    row_adapter_index,
    adapter_storage_slot,
):
    hidden = (
        jax.nn.silu(gate_preactivation.astype(jnp.float32)) * up_preactivation.astype(jnp.float32)
    ).astype(jnp.bfloat16)
    tensor_count = lax.axis_size("tensor")
    data_count = lax.axis_size("dp")
    adapter_count = adapter_storage_slot.shape[0]
    compare = row_adapter_index[:, None] == jnp.arange(adapter_count, dtype=jnp.int32)[None, :]
    slot = jnp.sum(jnp.where(compare, adapter_storage_slot[None, :], 0), axis=1)
    pieces_a, pieces_b = (
        lax.all_gather(adapter_input_maps, "dp", axis=0, tiled=True),
        lax.all_gather(adapter_output_maps, "dp", axis=0, tiled=True),
    )
    pieces_a, pieces_b = (
        lax.all_to_all(pieces_a, "tensor", split_axis=2, concat_axis=0, tiled=True),
        lax.all_to_all(pieces_b, "tensor", split_axis=2, concat_axis=0, tiled=True),
    )
    position = slot % tensor_count * data_count + slot // tensor_count
    row_storage_slots = pieces_a.shape[0]
    rank_projection = pieces_a.shape[1]
    onehot = position[:, None] == jnp.arange(row_storage_slots, dtype=jnp.int32)[None, :]
    flattened_input_maps = pieces_a.reshape(row_storage_slots * rank_projection, pieces_a.shape[2])
    inner = lax.dot_general(
        hidden, flattened_input_maps, (((1,), (1,)), ((), ())), preferred_element_type=jnp.float32
    )
    low_part = jnp.sum(
        inner.reshape(-1, row_storage_slots, rank_projection)
        * onehot[:, :, None].astype(jnp.float32),
        axis=1,
    )
    low_b = lax.psum(low_part.astype(jnp.bfloat16), "tensor")
    widened_rows = (onehot[:, :, None].astype(jnp.bfloat16) * low_b[:, None, :]).reshape(
        -1, row_storage_slots * rank_projection
    )
    adapter_output = jnp.dot(
        widened_rows,
        pieces_b.reshape(row_storage_slots * rank_projection, pieces_b.shape[2]),
        preferred_element_type=jnp.float32,
    )
    partial_out = jnp.dot(hidden, down_matrix, preferred_element_type=jnp.float32)
    base = lax.psum_scatter(
        partial_out.astype(jnp.bfloat16), "tensor", scatter_dimension=1, tiled=True
    ).astype(jnp.float32)
    return (base + adapter_output).astype(jnp.bfloat16)


def solution(mesh):
    placed = (
        P(("groups", "dp"), "tensor"),
        P(("groups", "dp"), "tensor"),
        P("tensor", None),
        P(("dp", "tensor"), None, None),
        P(("dp", "tensor"), None, None),
        P(("groups", "dp")),
        P(),
    )
    return jax.shard_map(
        local, mesh=mesh, in_specs=placed, out_specs=P(("groups", "dp"), "tensor"), check_vma=False
    )
```

profile of v0, /device:TPU:8, one launch (start us, length us, event | category | flops | bytes accessed | tf_op | source)
XLA Modules:
  0.0 506.3 jit_solution(11190234026428428343)
XLA Ops:
  6.5 0.7 all-gather.3.cloned.1.call-update
  7.3 16.8 %all-gather.3.cloned.1.call-done = bf16[2,64,16384]{2,1,0:T(8,128)(2,1)} async-done(((bf16[1,64,16384]{2,1,0:T(8,128)(2,1)}), bf16[2,64,16384]{2,1,0:T(8,128)(2,1)}) %all-gather.3.cloned.1.call-update) | async-done | bytes 4194320 | tf_op jit(solution)/shard_map/all_gather | solution.py:25
  24.0 17.8 %copy.18 = bf16[2,64,16384]{1,0,2:T(2,128)(2,1)} copy(bf16[2,64,16384]{2,1,0:T(8,128)(2,1)} %all-gather.3.cloned.1.call-done) | data formatting | bytes 8388608 | tf_op jit(solution)/shard_map/all_gather | solution.py:25
  41.8 10.5 %reshape.99 = bf16[8,2,131072]{2,1,0:T(2,128)(2,1)} reshape(bf16[16384,2,64]{2,1,0:T(2,128)(2,1)} %bitcast.23) | data formatting | bytes 8388608
  52.3 6.2 %all-to-all-start = ((bf16[8,2,131072]{2,1,0:T(2,128)(2,1)}), bf16[8,2,131072]{2,1,0:T(2,128)(2,1)}, u32[]{:S(2)}, u32[]{:S(2)}) async-start(bf16[8,2,131072]{2,1,0:T(2,128)(2,1)} %reshape.99), calls=%async_computation.1 | async-start | bytes 8388608 | tf_op jit(solution)/shard_map/all_to_all | solution.py:29
  58.5 0.7 all-gather.5.cloned.1.call-update
  59.2 0.0 all-reduce.2.cloned.1.call-start
  59.3 0.1 select_reduce_fusion
  59.4 90.3 %all-to-all-done = bf16[8,2,131072]{2,1,0:T(2,128)(2,1)} async-done(((bf16[8,2,131072]{2,1,0:T(2,128)(2,1)}), bf16[8,2,131072]{2,1,0:T(2,128)(2,1)}, u32[]{:S(2)}, u32[]{:S(2)}) %all-to-all-start) | async-done | bytes 4194336 | tf_op jit(solution)/shard_map/all_to_all | solution.py:29
  149.7 10.3 %reshape.100 = bf16[16384,2,64]{2,1,0:T(2,128)(2,1)} reshape(bf16[8,2,131072]{2,1,0:T(2,128)(2,1)} %all-to-all-done) | data formatting | bytes 8388608
  160.0 20.2 %copy.19 = bf16[2,64,8,2048]{3,1,0,2:T(8,128)(2,1)} copy(bf16[2,64,8,2048]{1,0,3,2:T(2,128)(2,1)} %bitcast.24) | data formatting | bytes 8388608 | tf_op jit(solution)/shard_map/all_to_all | solution.py:29
  180.2 8.3 %multiply_reduce_fusion = bf16[768,64]{0,1:T(8,128)(2,1)} fusion(bf16[16,64,2048]{2,1,0:T(8,128)(2,1)} %bitcast.27, f32[768,16]{0,1:T(8,128)S(1)} %get-tuple-element.6, bf16[768,2048]{1,0:T(8,128)(2,1)} %param.8, bf16[768,2048]{1,0:T(8,128)(2,1)} %param.7), kind=kOutput, calls=%fused_computation.11 | convolution fusion | flops 3235332096 | bytes 10633216 | tf_op jit(solution)/shard_map/dot_general | solution.py:37
  188.5 0.0 reduce-scatter.2.cloned.1.call-start
  188.6 35.2 %convolution_convert_fusion = bf16[768,8192]{1,0:T(8,128)(2,1)} fusion(bf16[2048,8192]{1,0:T(8,128)(2,1)} %param.9, bf16[768,2048]{1,0:T(8,128)(2,1)} %param.8, bf16[768,2048]{1,0:T(8,128)(2,1)} %param.7), kind=kOutput, calls=%fused_computation | convolution fusion | flops 25788678144 | bytes 52428800 | tf_op jit(solution)/shard_map/dot_general | solution.py:54
  223.8 0.0 all-gather.5.cloned.1.call-done
  223.8 9.5 %copy.20 = bf16[2,64,8192]{1,0,2:T(2,128)(2,1)} copy(bf16[2,64,8192]{2,1,0:T(8,128)(2,1)} %all-gather.5.cloned.1.call-done) | data formatting | bytes 4194304 | tf_op jit(solution)/shard_map/all_gather | solution.py:26
  233.4 6.4 %reshape.101 = bf16[8,2,65536]{2,1,0:T(2,128)(2,1)S(1)} reshape(bf16[8192,2,64]{2,1,0:T(2,128)(2,1)} %bitcast.25) | data formatting | bytes 4194304
  239.7 89.7 %all_to_all.30 = bf16[8,2,65536]{2,1,0:T(2,128)(2,1)} all-to-all(bf16[8,2,65536]{2,1,0:T(2,128)(2,1)S(1)} %reshape.101), channel_id=1, replica_groups=mesh['groups'=2,'dp'=2,'tensor'=8] {'tensor'}, dimensions={0} | all-to-all | bytes 4194304 | tf_op jit(solution)/shard_map/all_to_all | solution.py:30
  329.5 7.5 %reshape.102 = bf16[8192,2,64]{2,1,0:T(2,128)(2,1)} reshape(bf16[8,2,65536]{2,1,0:T(2,128)(2,1)} %all_to_all.30) | data formatting | bytes 4194304
  336.9 9.2 %copy.24 = bf16[2,64,8,1024]{3,1,0,2:T(8,128)(2,1)S(1)} copy(bf16[2,64,8,1024]{1,0,3,2:T(2,128)(2,1)} %bitcast.26) | data formatting | bytes 4194304 | tf_op jit(solution)/shard_map/all_to_all | solution.py:30
  346.1 0.0 all-reduce.2.cloned.1.call-done
  346.1 2.2 broadcast_multiply_fusion
  348.4 146.6 %reduce-scatter.2.cloned.1.call-done = bf16[768,1024]{1,0:T(8,128)(2,1)} async-done(((bf16[768,8192]{1,0:T(8,128)(2,1)}), bf16[768,1024]{1,0:T(8,128)(2,1)}) %reduce-scatter.2.cloned.1.call-update) | async-done | bytes 1572880 | tf_op jit(solution)/shard_map/reduce_scatter | solution.py:55
  494.9 4.9 add_convert_fusion
  (10 shorter events, 0.1 us)
Async XLA Ops:
  6.5 17.5 %all-gather.3.cloned.1.call-start = ((), (), s32[]{:S(2)}) async-start(), calls=%async_computation.4 | async-start | bytes 6291456 | tf_op jit(solution)/shard_map/all_gather | solution.py:25
  52.3 7.0 %copy-start = (s32[768]{0:T(1024)S(1)}, s32[768]{0:T(1024)}, u32[]{:S(2)}) copy-start(s32[768]{0:T(1024)} %param.12) | copy-start | bytes 9220
  52.3 7.0 %copy-start.1 = (s32[16]{0:T(128)S(1)}, s32[16]{0:T(128)}, u32[]{:S(2)}) copy-start(s32[16]{0:T(128)} %param.13) | copy-start | bytes 196
  52.3 97.4 %all-to-all-start = ((bf16[8,2,131072]{2,1,0:T(2,128)(2,1)}), bf16[8,2,131072]{2,1,0:T(2,128)(2,1)}, u32[]{:S(2)}, u32[]{:S(2)}) async-start(bf16[8,2,131072]{2,1,0:T(2,128)(2,1)} %reshape.99), calls=%async_computation.1 | async-start | bytes 8388608 | tf_op jit(solution)/shard_map/all_to_all | solution.py:29
  58.5 165.3 %all-gather.5.cloned.1.call-start = ((), (), s32[]{:S(2)}) async-start(), calls=%async_computation.6 | async-start | bytes 3145728 | tf_op jit(solution)/shard_map/all_gather | solution.py:26
  59.2 286.9 %all-reduce.2.cloned.1.call-start = ((), (), s32[]{:S(2)}) async-start(), calls=%async_computation.5 | async-start | bytes 196608 | tf_op jit(solution)/shard_map/psum | solution.py:45
  188.5 306.4 %reduce-scatter.2.cloned.1.call-start = ((), (), s32[]{:S(2)}) async-start(), calls=%async_computation.3 | async-start | bytes 14155776 | tf_op jit(solution)/shard_map/reduce_scatter | solution.py:55
Sparse Core Ops, SparseCore 0:
  8.9 15.0 all-gather.2
  60.9 11.6 all-gather.4
  188.6 70.7 all-reduce.1
  262.9 231.9 reduce-scatter.1
where the time goes:
time: 512 us; the launch traced here: 506 us
  waiting for transfers between devices  255 us (50%)
  local copies, waits for them, and re-layouts  91.4 us (18%)
  blocking collectives  89.7 us (18%)
  matrix products  48.3 us (9%)
  between operations  13.2 us (3%)
  starting transfers between devices  6.27 us (1%)
    reduce_scatter x1, waiting for transfers between devices, local(): lax.psum_scatter(partial_out.astype(jnp.bfloat16), 'tensor', scatter_dime...  147 us
    all_to_all x1, waiting for transfers between devices, local(): lax.all_to_all(pieces_a, 'tensor', split_axis=2, concat_axis=0, tiled=True)  90.3 us
    all_to_all x1, blocking collectives, local(): lax.all_to_all(pieces_b, 'tensor', split_axis=2, concat_axis=0, tiled=True)  89.7 us
    dot_general x1, matrix products, local(): jnp.dot(hidden, down_matrix, preferred_element_type=jnp.float32)  35.2 us
    unnamed x8, local copies, waits for them, and re-layouts  34.7 us
    all_to_all x1, local copies, waits for them, and re-layouts, local(): lax.all_to_all(pieces_a, 'tensor', split_axis=2, concat_axis=0, tiled=True)  20.2 us
    all_gather x1, local copies, waits for them, and re-layouts, local(): lax.all_gather(adapter_input_maps, 'dp', axis=0, tiled=True)  17.8 us
    all_gather x1, waiting for transfers between devices, local(): lax.all_gather(adapter_input_maps, 'dp', axis=0, tiled=True)  16.8 us
  transfers between devices with their start and end apart: 5, of which 3 were waited for; matrix products, arithmetic and copies ran while one was open for 22% of the time, Pallas kernels for 0%

commit v1 on v0

--- a/solution.py
+++ b/solution.py
@@ -1,7 +1,377 @@
+import functools
+
 import jax
 import jax.numpy as jnp
 from jax import lax
+from jax.experimental import pallas as pl
+from jax.experimental.pallas import tpu as pltpu
 from jax.sharding import PartitionSpec as P
+
+MESH = pl.DeviceIdType.MESH
+F32, BF16 = jnp.float32, jnp.bfloat16
+N_Y, N_Z = 2, 4
+CHUNKS = 4
+MESSAGES = CHUNKS * N_Z
+W_SLOTS = 4
+Y_LAG, HOP_LAG = 8, 2
+LOW_STEP, SUM_STEP = 8, 11
+STEPS = MESSAGES + Y_LAG + HOP_LAG * (N_Z - 1)
+
+
+def fused(
+    gate, up, w, a, b, pos, out,
+    hid, part, yrecv, zl, zr, wbuf, stage, aall, ball, lowr, wid,
+    y_s, y_r, z_s, zl_r, zr_r, w_sem, st_sem, a_s, a_r, b_s, b_r, l_s, l_r, dp_s, dp_r, own_sem,
+):
+    tensor = N_Y * N_Z
+    t = lax.axis_index("tensor")
+    d = lax.axis_index("dp")
+    z, y = t // N_Y, t % N_Y
+    rows, depth = hid.shape
+    block_cols = out.shape[1]
+    width = block_cols // CHUNKS
+    stage_rows = stage.shape[2]
+
+    def peer(k):
+        return lax.rem(t + k, tensor)
+
+    def z_of(m):
+        return lax.rem(3 * lax.rem(m, N_Z), N_Z)
+
+    def w_copy(j):
+        m, own = j // 2, lax.rem(j, 2)
+        y_dest = jnp.where(own == 1, y, 1 - y)
+        col = (z_of(m) * N_Y + y_dest) * block_cols + (m // N_Z) * width
+        slot = lax.rem(j, W_SLOTS)
+        return pltpu.make_async_copy(
+            w.at[:, pl.ds(pl.multiple_of(col, width), width)], wbuf.at[slot], w_sem.at[slot]
+        )
+
+    def stage_copies(i):
+        s = lax.rem(i, 2)
+        span = pl.ds(pl.multiple_of(i * stage_rows, stage_rows), stage_rows)
+        return [
+            pltpu.make_async_copy(src.at[span, :], stage.at[n, s], st_sem.at[n, s])
+            for n, src in enumerate((gate, up))
+        ]
+
+    def a_copy(source, dest):
+        return pltpu.make_async_remote_copy(
+            src_ref=a.at[0, :, pl.ds(pl.multiple_of(dest * depth, depth), depth)],
+            dst_ref=aall.at[d * tensor + source],
+            send_sem=a_s.at[dest], recv_sem=a_r.at[source],
+            device_id={"tensor": dest}, device_id_type=MESH,
+        )
+
+    def b_copy(source, dest):
+        return pltpu.make_async_remote_copy(
+            src_ref=b.at[0, :, pl.ds(pl.multiple_of(dest * block_cols, block_cols), block_cols)],
+            dst_ref=ball.at[d * tensor + source],
+            send_sem=b_s.at[dest], recv_sem=b_r.at[source],
+            device_id={"tensor": dest}, device_id_type=MESH,
+        )
+
+    def low_copy(source, dest):
+        return pltpu.make_async_remote_copy(
+            src_ref=lowr.at[source], dst_ref=lowr.at[source],
+            send_sem=l_s.at[dest], recv_sem=l_r.at[source],
+            device_id={"tensor": dest}, device_id_type=MESH,
+        )
+
+    def dp_copy(buf, n, half):
+        span = pl.ds(half * tensor, tensor)
+        return pltpu.make_async_remote_copy(
+            src_ref=buf.at[span], dst_ref=buf.at[span],
+            send_sem=dp_s.at[n], recv_sem=dp_r.at[n],
+            device_id={"dp": 1 - d}, device_id_type=MESH,
+        )
+
+    def y_copy(m):
+        return pltpu.make_async_remote_copy(
+            src_ref=part.at[0, m], dst_ref=yrecv.at[m],
+            send_sem=y_s.at[m], recv_sem=y_r.at[m],
+            device_id={"tensor": z * N_Y + 1 - y}, device_id_type=MESH,
+        )
+
+    def right_copy(m):
+        return pltpu.make_async_remote_copy(
+            src_ref=part.at[1, m], dst_ref=zl.at[m],
+            send_sem=z_s.at[m], recv_sem=zl_r.at[m],
+            device_id={"tensor": lax.rem(t + N_Y, tensor)}, device_id_type=MESH,
+        )
+
+    def left_copy(m):
+        return pltpu.make_async_remote_copy(
+            src_ref=part.at[1, m], dst_ref=zr.at[m],
+            send_sem=z_s.at[m], recv_sem=zr_r.at[m],
+            device_id={"tensor": lax.rem(t + tensor - N_Y, tensor)}, device_id_type=MESH,
+        )
+
+    for copy in stage_copies(0):
+        copy.start()
+
+    @pl.loop(0, W_SLOTS)
+    def _(j):
+        w_copy(j).start()
+
+    own_a = pltpu.make_async_copy(
+        a.at[0, :, pl.ds(pl.multiple_of(t * depth, depth), depth)], aall.at[d * tensor + t], own_sem.at[0]
+    )
+    own_b = pltpu.make_async_copy(
+        b.at[0, :, pl.ds(pl.multiple_of(t * block_cols, block_cols), block_cols)],
+        ball.at[d * tensor + t], own_sem.at[1],
+    )
+    own_a.start()
+    own_b.start()
+
+    barrier = pltpu.get_barrier_semaphore()
+
+    @pl.loop(1, tensor)
+    def _(k):
+        pl.semaphore_signal(barrier, inc=1, device_id={"tensor": peer(k)}, device_id_type=MESH)
+
+    pl.semaphore_signal(barrier, inc=1, device_id={"dp": 1 - d}, device_id_type=MESH)
+    pl.semaphore_wait(barrier, tensor)
+
+    @pl.loop(1, tensor)
+    def _(k):
+        a_copy(t, peer(k)).start()
+
+    @pl.loop(0, rows // stage_rows)
+    def _(i):
+        @pl.when(i + 1 < rows // stage_rows)
+        def _():
+            for copy in stage_copies(i + 1):
+                copy.start()
+
+        for copy in stage_copies(i):
+            copy.wait()
+        s = lax.rem(i, 2)
+        v = stage[0, s].astype(F32)
+        u = stage[1, s].astype(F32)
+        span = pl.ds(pl.multiple_of(i * stage_rows, stage_rows), stage_rows)
+        hid[span, :] = (v / (1.0 + jnp.exp(-v)) * u).astype(BF16)
+
+    def lanes(shape):
+        return lax.broadcasted_iota(jnp.int32, shape, 1)
+
+    four = 4 * aall.shape[1]
+    pair = 2 * aall.shape[1]
+    rank = aall.shape[1]
+
+    def low_of(first, acc):
+        def body(q, acc):
+            maps = aall[pl.ds(first + 4 * q, 4)].reshape(four, depth)
+            inner = lax.dot_general(hid[...], maps, (((1,), (1,)), ((), ())), preferred_element_type=F32)
+            wanted = jnp.concatenate([pos[...]] * 2, axis=1) == first + 4 * q + lanes(inner.shape) // rank
+            inner = jnp.where(wanted, inner, 0.0)
+            return acc + inner[:, :pair] + inner[:, pair:]
+
+        return lax.fori_loop(0, tensor // 4, body, acc)
+
+    half = rows // 2
+
+    @pl.loop(0, STEPS)
+    def _(s):
+        @pl.when(s < MESSAGES)
+        def _():
+            @pl.loop(0, 2)
+            def _(own):
+                j = 2 * s + own
+                w_copy(j).wait()
+                prod = jnp.dot(hid[...], wbuf[lax.rem(j, W_SLOTS)], preferred_element_type=F32)
+                part[own, s] = prod.astype(BF16)
+
+                @pl.when(j + W_SLOTS < 2 * MESSAGES)
+                def _():
+                    w_copy(j + W_SLOTS).start()
+
+                @pl.when(own == 0)
+                def _():
+                    y_copy(s).start()
+
+        @pl.when(s == 1)
+        def _():
+            @pl.loop(1, tensor)
+            def _(k):
+                b_copy(t, peer(k)).start()
+
+        @pl.when(s == LOW_STEP)
+        def _():
+            own_a.wait()
+
+            @pl.loop(1, tensor)
+            def _(k):
+                a_copy(peer(k), t).wait_recv()
+
+            dp_copy(aall, 0, d).start()
+            acc = low_of(d * tensor, jnp.zeros((rows, pair), F32))
+            dp_copy(aall, 0, 1 - d).wait_recv()
+            acc = low_of((1 - d) * tensor, acc)
+            both = acc + pltpu.roll(acc, rank, 1)
+            lowr[t] = jnp.where(lanes((half, pair)) < rank, both[:half], both[half:]).astype(BF16)
+
+            @pl.loop(1, tensor)
+            def _(k):
+                low_copy(t, peer(k)).start()
+
+        @pl.when(s == SUM_STEP)
+        def _():
+            own_b.wait()
+
+            @pl.loop(1, tensor)
+            def _(k):
+                b_copy(peer(k), t).wait_recv()
+
+            dp_copy(ball, 1, d).start()
+
+            @pl.loop(1, tensor)
+            def _(k):
+                low_copy(peer(k), t).wait_recv()
+
+            total = lowr[0].astype(F32)
+            for k in range(1, tensor):
+                total = total + lowr[k].astype(F32)
+            total = total.astype(BF16).astype(F32)
+            other = pltpu.roll(total, rank, 1)
+            low_lane = lanes(total.shape) < rank
+            upper = jnp.where(low_lane, total, other)
+            lower = jnp.where(low_lane, other, total)
+            for k in range(2 * tensor // 2):
+                for n, values in enumerate((upper, lower)):
+                    span = pl.ds(n * half, half)
+                    wanted = pos[span, :] == 2 * k + lanes(values.shape) // rank
+                    wid[span, pl.ds(k * pair, pair)] = jnp.where(wanted, values, 0.0).astype(BF16)
+            dp_copy(ball, 1, 1 - d).wait_recv()
+
+        mr = s - Y_LAG - HOP_LAG * z
+
+        @pl.when((mr >= 0) & (mr < MESSAGES))
+        def _():
+            @pl.when(z_of(mr) > z)
+            def _():
+                y_copy(mr).wait_recv()
+
+                @pl.when(z == 0)
+                def _():
+                    part[1, mr] = (part[1, mr].astype(F32) + yrecv[mr].astype(F32)).astype(BF16)
+
+                @pl.when(z > 0)
+                def _():
+                    right_copy(mr).wait_recv()
+                    part[1, mr] = (
+                        part[1, mr].astype(F32) + yrecv[mr].astype(F32) + zl[mr].astype(F32)
+                    ).astype(BF16)
+
+                right_copy(mr).start()
+
+        ml = s - Y_LAG - HOP_LAG * (N_Z - 1 - z)
+
+        @pl.when((ml >= 0) & (ml < MESSAGES))
+        def _():
+            @pl.when(z_of(ml) < z)
+            def _():
+                y_copy(ml).wait_recv()
+
+                @pl.when(z == N_Z - 1)
+                def _():
+                    part[1, ml] = (part[1, ml].astype(F32) + yrecv[ml].astype(F32)).astype(BF16)
+
+                @pl.when(z < N_Z - 1)
+                def _():
+                    left_copy(ml).wait_recv()
+                    part[1, ml] = (
+                        part[1, ml].astype(F32) + yrecv[ml].astype(F32) + zr[ml].astype(F32)
+                    ).astype(BF16)
+
+                left_copy(ml).start()
+
+        mf = s - Y_LAG - HOP_LAG * jnp.maximum(z, N_Z - 1 - z)
+
+        @pl.when((mf >= 0) & (mf < MESSAGES))
+        def _():
+            @pl.when(z_of(mf) == z)
+            def _():
+                y_copy(mf).wait_recv()
+                cols = pl.ds(pl.multiple_of((mf // N_Z) * width, width), width)
+                maps = ball[:, :, cols].reshape(2 * tensor * rank, width)
+                total = jnp.dot(wid[...], maps, preferred_element_type=F32)
+                total = total + part[1, mf].astype(F32) + yrecv[mf].astype(F32)
+
+                @pl.when(z == 0)
+                def _():
+                    left_copy(mf).wait_recv()
+                    out[:, cols] = (total + zr[mf].astype(F32)).astype(BF16)
+
+                @pl.when(z == N_Z - 1)
+                def _():
+                    right_copy(mf).wait_recv()
+                    out[:, cols] = (total + zl[mf].astype(F32)).astype(BF16)
+
+                @pl.when((z > 0) & (z < N_Z - 1))
+                def _():
+                    left_copy(mf).wait_recv()
+                    right_copy(mf).wait_recv()
+                    out[:, cols] = (total + zl[mf].astype(F32) + zr[mf].astype(F32)).astype(BF16)
+
+    @pl.loop(0, MESSAGES)
+    def _(m):
+        y_copy(m).wait_send()
+
+        @pl.when(z_of(m) != z)
+        def _():
+            right_copy(m).wait_send()
+
+    @pl.loop(1, tensor)
+    def _(k):
+        a_copy(t, peer(k)).wait_send()
+        b_copy(t, peer(k)).wait_send()
+        low_copy(t, peer(k)).wait_send()
+
+    dp_copy(aall, 0, d).wait_send()
+    dp_copy(ball, 1, d).wait_send()
+
+
+def local_fused(gate, up, w, a, b, row_adapter_index, adapter_storage_slot):
+    adapters = adapter_storage_slot.shape[0]
+    compare = row_adapter_index[:, None] == jnp.arange(adapters, dtype=jnp.int32)[None, :]
+    slot = jnp.sum(jnp.where(compare, adapter_storage_slot[None, :], 0), axis=1)
+    tensor = N_Y * N_Z
+    rows, depth = gate.shape
+    rank = a.shape[1]
+    block_cols = w.shape[1] // tensor
+    width = block_cols // CHUNKS
+    pos = jnp.broadcast_to(slot[:, None], (rows, 2 * rank))
+    stage_rows = 64
+    hbm = pl.BlockSpec(memory_space=pl.ANY)
+    vmem = pl.BlockSpec(memory_space=pltpu.VMEM)
+    dma = pltpu.SemaphoreType.DMA
+    return pl.pallas_call(
+        fused,
+        out_shape=jax.ShapeDtypeStruct((rows, block_cols), BF16),
+        in_specs=[hbm] * 5 + [vmem],
+        out_specs=vmem,
+        scratch_shapes=[
+            pltpu.VMEM((rows, depth), BF16),
+            pltpu.VMEM((2, MESSAGES, rows, width), BF16),
+            pltpu.VMEM((MESSAGES, rows, width), BF16),
+            pltpu.VMEM((MESSAGES, rows, width), BF16),
+            pltpu.VMEM((MESSAGES, rows, width), BF16),
+            pltpu.VMEM((W_SLOTS, depth, width), BF16),
+            pltpu.VMEM((2, 2, stage_rows, depth), BF16),
+            pltpu.VMEM((adapters, rank, depth), BF16),
+            pltpu.VMEM((adapters, rank, block_cols), BF16),
+            pltpu.VMEM((tensor, rows // 2, 2 * rank), BF16),
+            pltpu.VMEM((rows, adapters * rank), BF16),
+            dma((MESSAGES,)), dma((MESSAGES,)), dma((MESSAGES,)), dma((MESSAGES,)), dma((MESSAGES,)),
+            dma((W_SLOTS,)), dma((2, 2)),
+            dma((tensor,)), dma((tensor,)), dma((tensor,)), dma((tensor,)), dma((tensor,)), dma((tensor,)),
+            dma((2,)), dma((2,)), dma((2,)),
+        ],
+        compiler_params=pltpu.CompilerParams(
+            collective_id=0, has_side_effects=True, vmem_limit_bytes=60 * 1024 * 1024
+        ),
+    )(gate, up, w, a, b, pos)
 
 
 def local(
@@ -68,6 +438,8 @@
         P(("groups", "dp")),
         P(),
     )
+    sizes = dict(mesh.shape)
+    fits = sizes["tensor"] == N_Y * N_Z and sizes["dp"] == 2
     return jax.shard_map(
-        local, mesh=mesh, in_specs=placed, out_specs=P(("groups", "dp"), "tensor"), check_vma=False
-    )
+        local_fused if fits else local, mesh=mesh, in_specs=placed, out_specs=P(("groups", "dp"), "tensor"), check_vma=False
+    )

time: 512 us -> 228 us (0.45)
  waiting for transfers between devices: 255 us -> 0 us
  Pallas kernels: 0 us -> 221 us
  blocking collectives: 89.7 us -> 0 us
  local copies, waits for them, and re-layouts: 91.4 us -> 3.58 us
  matrix products: 48.3 us -> 0 us
  between operations: 13.2 us -> 0.01 us
  starting transfers between devices: 6.27 us -> 0 us
    pallas_call x0 -> x1, Pallas kernels: none -> 221 us  [local_fused(): pl.pallas_call(fused, out_shape=jax.ShapeDtypeStruct((rows, block_cols),...]
    reduce_scatter x1 -> x0, waiting for transfers between devices: 147 us -> none  [local(): lax.psum_scatter(partial_out.astype(jnp.bfloat16), 'tensor', scatter_dime...]
    all_to_all x1 -> x0, waiting for transfers between devices: 90.3 us -> none  [local(): lax.all_to_all(pieces_a, 'tensor', split_axis=2, concat_axis=0, tiled=True)]
    all_to_all x1 -> x0, blocking collectives: 89.7 us -> none  [local(): lax.all_to_all(pieces_b, 'tensor', split_axis=2, concat_axis=0, tiled=True)]
    dot_general x3 -> x0, matrix products: 48.3 us -> none  [the longest x1 35.2 us: local(): jnp.dot(hidden, down_matrix, preferred_element_type=jnp.float32)]
    unnamed x8 -> x1, local copies, waits for them, and re-layouts: 34.7 us -> 2.67 us
    all_to_all x2 -> x0, local copies, waits for them, and re-layouts: 29.4 us -> none  [the longest x1 20.2 us: local(): lax.all_to_all(pieces_a, 'tensor', split_axis=2, concat_axis=0, tiled=True)]
    all_gather x2 -> x0, local copies, waits for them, and re-layouts: 27.3 us -> none  [the longest x1 17.8 us: local(): lax.all_gather(adapter_input_maps, 'dp', axis=0, tiled=True)]
  transfers between devices with their start and end apart: 5 -> 0, of which waited for: 3 -> 0; matrix products, arithmetic and copies ran while one was open for 22% -> 0% of each run, Pallas kernels for 0% -> 0%
where the time goes in v1:
time: 228 us; the launch traced here: 226 us
  Pallas kernels  221 us (97%)
  local copies, waits for them, and re-layouts  3.58 us (2%)
    pallas_call x1, Pallas kernels, local_fused(): pl.pallas_call(fused, out_shape=jax.ShapeDtypeStruct((rows, block_cols),...  221 us

profile of v1, /device:TPU:8, one launch (start us, length us, event | category | flops | bytes accessed | tf_op | source)
XLA Modules:
  0.0 225.9 jit_solution(17507461406903206181)
XLA Ops:
  0.0 0.8 select_reduce_fusion
  0.8 0.9 broadcast_in_dim.23.pos
  1.7 221.5 %shard_map.73 = bf16[768,1024]{1,0:T(8,128)(2,1)} custom-call(bf16[768,2048]{1,0:T(8,128)(2,1)} %gate.1, bf16[768,2048]{1,0:T(8,128)(2,1)} %up.1, bf16[2048,8192]{1,0:T(8,128)(2,1)} %w.1, bf16[1,64,16384]{2,1,0:T(8,128)(2,1)} %a.1, bf16[1,64,8192]{2,1,0:T(8,128)(2,1)} %b.1, s32[768,128]{1,0:T(8,128)} %broadcast_in_dim.23.pos), custom_call_target="tpu_custom_call" | custom-call | tf_op jit(solution)/shard_map/pallas_call | solution.py:349
  223.2 2.7 %copy.9 = bf16[768,1024]{1,0:T(8,128)(2,1)} copy(bf16[768,1024]{1,0:T(8,128)(2,1)} %shard_map.73) | data formatting | bytes 3145728

commit v2 on v1

--- a/solution.py
+++ b/solution.py
@@ -11,37 +11,49 @@
 F32, BF16 = jnp.float32, jnp.bfloat16
 N_Y, N_Z = 2, 4
 CHUNKS = 4
-MESSAGES = CHUNKS * N_Z
+PARTS = 2
+MESSAGES = CHUNKS * N_Z * PARTS
 W_SLOTS = 4
-Y_LAG, HOP_LAG = 8, 2
-LOW_STEP, SUM_STEP = 8, 11
-STEPS = MESSAGES + Y_LAG + HOP_LAG * (N_Z - 1)
+Y_LAG, HOP_LAG = 10, 3
+LOW_STEP, PAIR_STEP, SUM_STEP, FINAL_LAG = 18, 21, 24, 25
+STEPS = MESSAGES + FINAL_LAG
 
 
 def fused(
     gate, up, w, a, b, pos, out,
-    hid, part, yrecv, zl, zr, wbuf, stage, aall, ball, lowr, wid,
-    y_s, y_r, z_s, zl_r, zr_r, w_sem, st_sem, a_s, a_r, b_s, b_r, l_s, l_r, dp_s, dp_r, own_sem,
+    hid, part, yrecv, zl, zr, wbuf, stage, aall, ball, lowy, lowz, wid,
+    y_s, y_r, z_s, zl_r, zr_r, w_sem, st_sem, a_s, a_r, b_s, b_r, ax_s, ax_r, bx_s, bx_r,
+    ly_s, ly_r, lz_s, lz_r, dp_s, dp_r, own_sem,
 ):
     tensor = N_Y * N_Z
     t = lax.axis_index("tensor")
     d = lax.axis_index("dp")
+    g = lax.axis_index("groups")
     z, y = t // N_Y, t % N_Y
     rows, depth = hid.shape
     block_cols = out.shape[1]
     width = block_cols // CHUNKS
     stage_rows = stage.shape[2]
+    part_rows = rows // PARTS
 
     def peer(k):
         return lax.rem(t + k, tensor)
 
     def z_of(m):
-        return lax.rem(3 * lax.rem(m, N_Z), N_Z)
+        return lax.rem(3 * lax.rem(m // PARTS, N_Z), N_Z)
+
+    def place(m):
+        col = pl.multiple_of(m // (N_Z * PARTS) * width, width)
+        row = pl.multiple_of(lax.rem(m, PARTS) * part_rows, part_rows)
+        return pl.ds(row, part_rows), pl.ds(col, width)
+
+    rank = aall.shape[1]
+    mine = pl.ds(pl.multiple_of(g * (rank // 2), rank // 2), rank // 2)
 
     def w_copy(j):
-        m, own = j // 2, lax.rem(j, 2)
+        m, own = j // 2 * PARTS, lax.rem(j, 2)
         y_dest = jnp.where(own == 1, y, 1 - y)
-        col = (z_of(m) * N_Y + y_dest) * block_cols + (m // N_Z) * width
+        col = (z_of(m) * N_Y + y_dest) * block_cols + m // (N_Z * PARTS) * width
         slot = lax.rem(j, W_SLOTS)
         return pltpu.make_async_copy(
             w.at[:, pl.ds(pl.multiple_of(col, width), width)], wbuf.at[slot], w_sem.at[slot]
@@ -57,25 +69,39 @@
 
     def a_copy(source, dest):
         return pltpu.make_async_remote_copy(
-            src_ref=a.at[0, :, pl.ds(pl.multiple_of(dest * depth, depth), depth)],
-            dst_ref=aall.at[d * tensor + source],
+            src_ref=a.at[0, mine, pl.ds(pl.multiple_of(dest * depth, depth), depth)],
+            dst_ref=aall.at[d * tensor + source, mine],
             send_sem=a_s.at[dest], recv_sem=a_r.at[source],
             device_id={"tensor": dest}, device_id_type=MESH,
         )
 
     def b_copy(source, dest):
         return pltpu.make_async_remote_copy(
-            src_ref=b.at[0, :, pl.ds(pl.multiple_of(dest * block_cols, block_cols), block_cols)],
-            dst_ref=ball.at[d * tensor + source],
+            src_ref=b.at[0, mine, pl.ds(pl.multiple_of(dest * block_cols, block_cols), block_cols)],
+            dst_ref=ball.at[d * tensor + source, mine],
             send_sem=b_s.at[dest], recv_sem=b_r.at[source],
             device_id={"tensor": dest}, device_id_type=MESH,
         )
 
-    def low_copy(source, dest):
-        return pltpu.make_async_remote_copy(
-            src_ref=lowr.at[source], dst_ref=lowr.at[source],
-            send_sem=l_s.at[dest], recv_sem=l_r.at[source],
-            device_id={"tensor": dest}, device_id_type=MESH,
+    def x_copy(buf, send, recv, source, half):
+        span = pl.ds(pl.multiple_of(half * (rank // 2), rank // 2), rank // 2)
+        return pltpu.make_async_remote_copy(
+            src_ref=buf.at[d * tensor + source, span], dst_ref=buf.at[d * tensor + source, span],
+            send_sem=send.at[source], recv_sem=recv.at[source],
+            device_id={"groups": 1 - g}, device_id_type=MESH,
+        )
+
+    def low_y_copy():
+        return pltpu.make_async_remote_copy(
+            src_ref=lowy.at[0], dst_ref=lowy.at[1], send_sem=ly_s.at[0], recv_sem=ly_r.at[0],
+            device_id={"tensor": z * N_Y + 1 - y}, device_id_type=MESH,
+        )
+
+    def low_z_copy(source, dest):
+        return pltpu.make_async_remote_copy(
+            src_ref=lowz.at[source], dst_ref=lowz.at[source],
+            send_sem=lz_s.at[dest], recv_sem=lz_r.at[source],
+            device_id={"tensor": dest * N_Y + y}, device_id_type=MESH,
         )
 
     def dp_copy(buf, n, half):
@@ -115,11 +141,12 @@
         w_copy(j).start()
 
     own_a = pltpu.make_async_copy(
-        a.at[0, :, pl.ds(pl.multiple_of(t * depth, depth), depth)], aall.at[d * tensor + t], own_sem.at[0]
+        a.at[0, mine, pl.ds(pl.multiple_of(t * depth, depth), depth)],
+        aall.at[d * tensor + t, mine], own_sem.at[0],
     )
     own_b = pltpu.make_async_copy(
-        b.at[0, :, pl.ds(pl.multiple_of(t * block_cols, block_cols), block_cols)],
-        ball.at[d * tensor + t], own_sem.at[1],
+        b.at[0, mine, pl.ds(pl.multiple_of(t * block_cols, block_cols), block_cols)],
+        ball.at[d * tensor + t, mine], own_sem.at[1],
     )
     own_a.start()
     own_b.start()
@@ -131,11 +158,16 @@
         pl.semaphore_signal(barrier, inc=1, device_id={"tensor": peer(k)}, device_id_type=MESH)
 
     pl.semaphore_signal(barrier, inc=1, device_id={"dp": 1 - d}, device_id_type=MESH)
-    pl.semaphore_wait(barrier, tensor)
+    pl.semaphore_signal(barrier, inc=1, device_id={"groups": 1 - g}, device_id_type=MESH)
+    pl.semaphore_wait(barrier, tensor + 1)
 
     @pl.loop(1, tensor)
     def _(k):
         a_copy(t, peer(k)).start()
+
+    @pl.loop(1, tensor)
+    def _(k):
+        b_copy(t, peer(k)).start()
 
     @pl.loop(0, rows // stage_rows)
     def _(i):
@@ -157,7 +189,6 @@
 
     four = 4 * aall.shape[1]
     pair = 2 * aall.shape[1]
-    rank = aall.shape[1]
 
     def low_of(first, acc):
         def body(q, acc):
@@ -173,65 +204,81 @@
 
     @pl.loop(0, STEPS)
     def _(s):
-        @pl.when(s < MESSAGES)
+        @pl.when((s < MESSAGES) & (lax.rem(s, PARTS) == 0))
         def _():
             @pl.loop(0, 2)
             def _(own):
-                j = 2 * s + own
+                j = s // PARTS * 2 + own
                 w_copy(j).wait()
                 prod = jnp.dot(hid[...], wbuf[lax.rem(j, W_SLOTS)], preferred_element_type=F32)
-                part[own, s] = prod.astype(BF16)
-
-                @pl.when(j + W_SLOTS < 2 * MESSAGES)
+                part[own, pl.ds(s, PARTS)] = prod.astype(BF16).reshape(PARTS, part_rows, width)
+
+                @pl.when(j + W_SLOTS < 2 * MESSAGES // PARTS)
                 def _():
                     w_copy(j + W_SLOTS).start()
 
                 @pl.when(own == 0)
                 def _():
-                    y_copy(s).start()
-
-        @pl.when(s == 1)
-        def _():
+                    for n in range(PARTS):
+                        y_copy(s + n).start()
+
+        @pl.when(s == 0)
+        def _():
+            own_a.wait()
+            x_copy(aall, ax_s, ax_r, t, g).start()
+
+        @pl.when((s >= 2) & (s < 2 * tensor) & (lax.rem(s, 2) == 0))
+        def _():
+            source = peer(s // 2)
+            a_copy(source, t).wait_recv()
+            x_copy(aall, ax_s, ax_r, source, g).start()
+
+        @pl.when(s == LOW_STEP)
+        def _():
+            own_b.wait()
+            x_copy(ball, bx_s, bx_r, t, g).start()
+
             @pl.loop(1, tensor)
             def _(k):
-                b_copy(t, peer(k)).start()
-
-        @pl.when(s == LOW_STEP)
-        def _():
-            own_a.wait()
-
-            @pl.loop(1, tensor)
+                b_copy(peer(k), t).wait_recv()
+                x_copy(ball, bx_s, bx_r, peer(k), g).start()
+
+            @pl.loop(0, tensor)
             def _(k):
-                a_copy(peer(k), t).wait_recv()
+                x_copy(aall, ax_s, ax_r, k, 1 - g).wait_recv()
 
             dp_copy(aall, 0, d).start()
             acc = low_of(d * tensor, jnp.zeros((rows, pair), F32))
             dp_copy(aall, 0, 1 - d).wait_recv()
             acc = low_of((1 - d) * tensor, acc)
             both = acc + pltpu.roll(acc, rank, 1)
-            lowr[t] = jnp.where(lanes((half, pair)) < rank, both[:half], both[half:]).astype(BF16)
-
-            @pl.loop(1, tensor)
+            lowy[0] = jnp.where(lanes((half, pair)) < rank, both[:half], both[half:]).astype(BF16)
+            low_y_copy().start()
+
+        @pl.when(s == PAIR_STEP)
+        def _():
+            low_y_copy().wait_recv()
+            lowz[z] = (lowy[0].astype(F32) + lowy[1].astype(F32)).astype(BF16)
+
+            @pl.loop(1, N_Z)
             def _(k):
-                low_copy(t, peer(k)).start()
+                low_z_copy(z, lax.rem(z + k, N_Z)).start()
+
+            @pl.loop(0, tensor)
+            def _(k):
+                x_copy(ball, bx_s, bx_r, k, 1 - g).wait_recv()
+
+            dp_copy(ball, 1, d).start()
 
         @pl.when(s == SUM_STEP)
         def _():
-            own_b.wait()
-
-            @pl.loop(1, tensor)
+            @pl.loop(1, N_Z)
             def _(k):
-                b_copy(peer(k), t).wait_recv()
-
-            dp_copy(ball, 1, d).start()
-
-            @pl.loop(1, tensor)
-            def _(k):
-                low_copy(peer(k), t).wait_recv()
-
-            total = lowr[0].astype(F32)
-            for k in range(1, tensor):
-                total = total + lowr[k].astype(F32)
+                low_z_copy(lax.rem(z + k, N_Z), z).wait_recv()
+
+            total = lowz[0].astype(F32)
+            for k in range(1, N_Z):
+                total = total + lowz[k].astype(F32)
             total = total.astype(BF16).astype(F32)
             other = pltpu.roll(total, rank, 1)
             low_lane = lanes(total.shape) < rank
@@ -286,33 +333,33 @@
 
                 left_copy(ml).start()
 
-        mf = s - Y_LAG - HOP_LAG * jnp.maximum(z, N_Z - 1 - z)
+        mf = s - FINAL_LAG
 
         @pl.when((mf >= 0) & (mf < MESSAGES))
         def _():
             @pl.when(z_of(mf) == z)
             def _():
                 y_copy(mf).wait_recv()
-                cols = pl.ds(pl.multiple_of((mf // N_Z) * width, width), width)
+                span, cols = place(mf)
                 maps = ball[:, :, cols].reshape(2 * tensor * rank, width)
-                total = jnp.dot(wid[...], maps, preferred_element_type=F32)
+                total = jnp.dot(wid[span, :], maps, preferred_element_type=F32)
                 total = total + part[1, mf].astype(F32) + yrecv[mf].astype(F32)
 
                 @pl.when(z == 0)
                 def _():
                     left_copy(mf).wait_recv()
-                    out[:, cols] = (total + zr[mf].astype(F32)).astype(BF16)
+                    out[span, cols] = (total + zr[mf].astype(F32)).astype(BF16)
 
                 @pl.when(z == N_Z - 1)
                 def _():
                     right_copy(mf).wait_recv()
-                    out[:, cols] = (total + zl[mf].astype(F32)).astype(BF16)
+                    out[span, cols] = (total + zl[mf].astype(F32)).astype(BF16)
 
                 @pl.when((z > 0) & (z < N_Z - 1))
                 def _():
                     left_copy(mf).wait_recv()
                     right_copy(mf).wait_recv()
-                    out[:, cols] = (total + zl[mf].astype(F32) + zr[mf].astype(F32)).astype(BF16)
+                    out[span, cols] = (total + zl[mf].astype(F32) + zr[mf].astype(F32)).astype(BF16)
 
     @pl.loop(0, MESSAGES)
     def _(m):
@@ -326,8 +373,17 @@
     def _(k):
         a_copy(t, peer(k)).wait_send()
         b_copy(t, peer(k)).wait_send()
-        low_copy(t, peer(k)).wait_send()
-
+
+    @pl.loop(0, tensor)
+    def _(k):
+        x_copy(aall, ax_s, ax_r, k, g).wait_send()
+        x_copy(ball, bx_s, bx_r, k, g).wait_send()
+
+    @pl.loop(1, N_Z)
+    def _(k):
+        low_z_copy(z, lax.rem(z + k, N_Z)).wait_send()
+
+    low_y_copy().wait_send()
     dp_copy(aall, 0, d).wait_send()
     dp_copy(ball, 1, d).wait_send()
 
@@ -353,19 +409,22 @@
         out_specs=vmem,
         scratch_shapes=[
             pltpu.VMEM((rows, depth), BF16),
-            pltpu.VMEM((2, MESSAGES, rows, width), BF16),
-            pltpu.VMEM((MESSAGES, rows, width), BF16),
-            pltpu.VMEM((MESSAGES, rows, width), BF16),
-            pltpu.VMEM((MESSAGES, rows, width), BF16),
+            pltpu.VMEM((2, MESSAGES, rows // PARTS, width), BF16),
+            pltpu.VMEM((MESSAGES, rows // PARTS, width), BF16),
+            pltpu.VMEM((MESSAGES, rows // PARTS, width), BF16),
+            pltpu.VMEM((MESSAGES, rows // PARTS, width), BF16),
             pltpu.VMEM((W_SLOTS, depth, width), BF16),
             pltpu.VMEM((2, 2, stage_rows, depth), BF16),
             pltpu.VMEM((adapters, rank, depth), BF16),
             pltpu.VMEM((adapters, rank, block_cols), BF16),
-            pltpu.VMEM((tensor, rows // 2, 2 * rank), BF16),
+            pltpu.VMEM((2, rows // 2, 2 * rank), BF16),
+            pltpu.VMEM((N_Z, rows // 2, 2 * rank), BF16),
             pltpu.VMEM((rows, adapters * rank), BF16),
             dma((MESSAGES,)), dma((MESSAGES,)), dma((MESSAGES,)), dma((MESSAGES,)), dma((MESSAGES,)),
             dma((W_SLOTS,)), dma((2, 2)),
-            dma((tensor,)), dma((tensor,)), dma((tensor,)), dma((tensor,)), dma((tensor,)), dma((tensor,)),
+            dma((tensor,)), dma((tensor,)), dma((tensor,)), dma((tensor,)),
+            dma((tensor,)), dma((tensor,)), dma((tensor,)), dma((tensor,)),
+            dma((1,)), dma((1,)), dma((N_Z,)), dma((N_Z,)),
             dma((2,)), dma((2,)), dma((2,)),
         ],
         compiler_params=pltpu.CompilerParams(
@@ -439,7 +498,7 @@
         P(),
     )
     sizes = dict(mesh.shape)
-    fits = sizes["tensor"] == N_Y * N_Z and sizes["dp"] == 2
+    fits = sizes["tensor"] == N_Y * N_Z and sizes["dp"] == 2 and sizes["groups"] == 2
     return jax.shard_map(
         local_fused if fits else local, mesh=mesh, in_specs=placed, out_specs=P(("groups", "dp"), "tensor"), check_vma=False
     )

time: 228 us -> 200 us (0.88)
  Pallas kernels: 221 us -> 194 us
    pallas_call x1, Pallas kernels: 221 us -> 194 us  [local_fused(): pl.pallas_call(fused, out_shape=jax.ShapeDtypeStruct((rows, block_cols),...]
where the time goes in v2:
time: 200 us; the launch traced here: 199 us
  Pallas kernels  194 us (97%)
  local copies, waits for them, and re-layouts  3.58 us (2%)
    pallas_call x1, Pallas kernels, local_fused(): pl.pallas_call(fused, out_shape=jax.ShapeDtypeStruct((rows, block_cols),...  194 us

profile of v2, /device:TPU:8, one launch (start us, length us, event | category | flops | bytes accessed | tf_op | source)
XLA Modules:
  0.0 198.8 jit_solution(18419418931047273191)
XLA Ops:
  0.0 0.8 select_reduce_fusion
  0.8 0.9 broadcast_in_dim.23.pos
  1.7 194.5 %shard_map.73 = bf16[768,1024]{1,0:T(8,128)(2,1)} custom-call(bf16[768,2048]{1,0:T(8,128)(2,1)} %gate.1, bf16[768,2048]{1,0:T(8,128)(2,1)} %up.1, bf16[2048,8192]{1,0:T(8,128)(2,1)} %w.1, bf16[1,64,16384]{2,1,0:T(8,128)(2,1)} %a.1, bf16[1,64,8192]{2,1,0:T(8,128)(2,1)} %b.1, s32[768,128]{1,0:T(8,128)} %broadcast_in_dim.23.pos), custom_call_target="tpu_custom_call" | custom-call | tf_op jit(solution)/shard_map/pallas_call | solution.py:405
  196.2 2.7 %copy.9 = bf16[768,1024]{1,0:T(8,128)(2,1)} copy(bf16[768,1024]{1,0:T(8,128)(2,1)} %shard_map.73) | data formatting | bytes 3145728

commit v3 on v2

--- a/solution.py
+++ b/solution.py
@@ -14,7 +14,7 @@
 PARTS = 2
 MESSAGES = CHUNKS * N_Z * PARTS
 W_SLOTS = 4
-Y_LAG, HOP_LAG = 10, 3
+Y_LAG, HOP_LAG = 3, 2
 LOW_STEP, PAIR_STEP, SUM_STEP, FINAL_LAG = 18, 21, 24, 25
 STEPS = MESSAGES + FINAL_LAG
 
@@ -227,9 +227,9 @@
             own_a.wait()
             x_copy(aall, ax_s, ax_r, t, g).start()
 
-        @pl.when((s >= 2) & (s < 2 * tensor) & (lax.rem(s, 2) == 0))
-        def _():
-            source = peer(s // 2)
+        @pl.when((s >= 6) & (s < 6 + tensor - 1))
+        def _():
+            source = peer(s - 5)
             a_copy(source, t).wait_recv()
             x_copy(aall, ax_s, ax_r, source, g).start()
 

time: 200 us -> 180 us (0.900)
  Pallas kernels: 194 us -> 176 us
    pallas_call x1, Pallas kernels: 194 us -> 176 us  [local_fused(): pl.pallas_call(fused, out_shape=jax.ShapeDtypeStruct((rows, block_cols),...]
where the time goes in v3:
time: 180 us
  Pallas kernels  176 us (98%)
  local copies, waits for them, and re-layouts  3.58 us (2%)
    pallas_call x1, Pallas kernels, local_fused(): pl.pallas_call(fused, out_shape=jax.ShapeDtypeStruct((rows, block_cols),...  176 us

profile of v3, /device:TPU:8, one launch (start us, length us, event | category | flops | bytes accessed | tf_op | source)
XLA Modules:
  0.0 179.9 jit_solution(4808187078500417245)
XLA Ops:
  0.0 0.8 select_reduce_fusion
  0.8 0.9 broadcast_in_dim.23.pos
  1.7 175.5 %shard_map.73 = bf16[768,1024]{1,0:T(8,128)(2,1)} custom-call(bf16[768,2048]{1,0:T(8,128)(2,1)} %gate.1, bf16[768,2048]{1,0:T(8,128)(2,1)} %up.1, bf16[2048,8192]{1,0:T(8,128)(2,1)} %w.1, bf16[1,64,16384]{2,1,0:T(8,128)(2,1)} %a.1, bf16[1,64,8192]{2,1,0:T(8,128)(2,1)} %b.1, s32[768,128]{1,0:T(8,128)} %broadcast_in_dim.23.pos), custom_call_target="tpu_custom_call" | custom-call | tf_op jit(solution)/shard_map/pallas_call | solution.py:405
  177.3 2.7 %copy.9 = bf16[768,1024]{1,0:T(8,128)(2,1)} copy(bf16[768,1024]{1,0:T(8,128)(2,1)} %shard_map.73) | data formatting | bytes 3145728

commit v4 on v3

--- a/solution.py
+++ b/solution.py
@@ -15,14 +15,16 @@
 MESSAGES = CHUNKS * N_Z * PARTS
 W_SLOTS = 4
 Y_LAG, HOP_LAG = 3, 2
+Z_FIRST = 1
+Z_SUM_LAG = Y_LAG + HOP_LAG * (N_Z - 1) + 2
 LOW_STEP, PAIR_STEP, SUM_STEP, FINAL_LAG = 18, 21, 24, 25
 STEPS = MESSAGES + FINAL_LAG
 
 
 def fused(
     gate, up, w, a, b, pos, out,
-    hid, part, yrecv, zl, zr, wbuf, stage, aall, ball, lowy, lowz, wid,
-    y_s, y_r, z_s, zl_r, zr_r, w_sem, st_sem, a_s, a_r, b_s, b_r, ax_s, ax_r, bx_s, bx_r,
+    hid, part, yrecv, zl, zr, zl2, zr2, wbuf, stage, aall, ball, lowy, lowz, wid,
+    y_s, y_r, z_s, zl_r, zr_r, z2_s, zl2_r, zr2_r, w_sem, st_sem, a_s, a_r, b_s, b_r, ax_s, ax_r, bx_s, bx_r,
     ly_s, ly_r, lz_s, lz_r, dp_s, dp_r, own_sem,
 ):
     tensor = N_Y * N_Z
@@ -42,6 +44,9 @@
     def z_of(m):
         return lax.rem(3 * lax.rem(m // PARTS, N_Z), N_Z)
 
+    def z_first(m):
+        return (m // (N_Z * PARTS) == Z_FIRST) & (lax.rem(m, PARTS) == PARTS - 1)
+
     def place(m):
         col = pl.multiple_of(m // (N_Z * PARTS) * width, width)
         row = pl.multiple_of(lax.rem(m, PARTS) * part_rows, part_rows)
@@ -133,6 +138,25 @@
             device_id={"tensor": lax.rem(t + tensor - N_Y, tensor)}, device_id_type=MESH,
         )
 
+    def right_other(m):
+        n = lax.rem(m // PARTS, N_Z)
+        return pltpu.make_async_remote_copy(
+            src_ref=part.at[0, m], dst_ref=zl2.at[n],
+            send_sem=z2_s.at[n], recv_sem=zl2_r.at[n],
+            device_id={"tensor": lax.rem(t + N_Y, tensor)}, device_id_type=MESH,
+        )
+
+    def left_other(m):
+        n = lax.rem(m // PARTS, N_Z)
+        return pltpu.make_async_remote_copy(
+            src_ref=part.at[0, m], dst_ref=zr2.at[n],
+            send_sem=z2_s.at[n], recv_sem=zr2_r.at[n],
+            device_id={"tensor": lax.rem(t + tensor - N_Y, tensor)}, device_id_type=MESH,
+        )
+
+    def add_to(own, m, buf, n):
+        part[own, m] = (part[own, m].astype(F32) + buf[n].astype(F32)).astype(BF16)
+
     for copy in stage_copies(0):
         copy.start()
 
@@ -220,7 +244,9 @@
                 @pl.when(own == 0)
                 def _():
                     for n in range(PARTS):
-                        y_copy(s + n).start()
+                        @pl.when(jnp.logical_not(z_first(s + n)))
+                        def _():
+                            y_copy(s + n).start()
 
         @pl.when(s == 0)
         def _():
@@ -297,18 +323,33 @@
         def _():
             @pl.when(z_of(mr) > z)
             def _():
-                y_copy(mr).wait_recv()
-
-                @pl.when(z == 0)
-                def _():
-                    part[1, mr] = (part[1, mr].astype(F32) + yrecv[mr].astype(F32)).astype(BF16)
-
-                @pl.when(z > 0)
-                def _():
-                    right_copy(mr).wait_recv()
-                    part[1, mr] = (
-                        part[1, mr].astype(F32) + yrecv[mr].astype(F32) + zl[mr].astype(F32)
-                    ).astype(BF16)
+                early = z_first(mr)
+
+                @pl.when(early)
+                def _():
+                    @pl.when(z > 0)
+                    def _():
+                        right_copy(mr).wait_recv()
+                        add_to(1, mr, zl, mr)
+                        right_other(mr).wait_recv()
+                        add_to(0, mr, zl2, lax.rem(mr // PARTS, N_Z))
+
+                    right_other(mr).start()
+
+                @pl.when(jnp.logical_not(early))
+                def _():
+                    y_copy(mr).wait_recv()
+
+                    @pl.when(z == 0)
+                    def _():
+                        add_to(1, mr, yrecv, mr)
+
+                    @pl.when(z > 0)
+                    def _():
+                        right_copy(mr).wait_recv()
+                        part[1, mr] = (
+                            part[1, mr].astype(F32) + yrecv[mr].astype(F32) + zl[mr].astype(F32)
+                        ).astype(BF16)
 
                 right_copy(mr).start()
 
@@ -318,20 +359,63 @@
         def _():
             @pl.when(z_of(ml) < z)
             def _():
-                y_copy(ml).wait_recv()
+                early = z_first(ml)
+
+                @pl.when(early)
+                def _():
+                    @pl.when(z < N_Z - 1)
+                    def _():
+                        left_copy(ml).wait_recv()
+                        add_to(1, ml, zr, ml)
+                        left_other(ml).wait_recv()
+                        add_to(0, ml, zr2, lax.rem(ml // PARTS, N_Z))
+
+                    left_other(ml).start()
+
+                @pl.when(jnp.logical_not(early))
+                def _():
+                    y_copy(ml).wait_recv()
+
+                    @pl.when(z == N_Z - 1)
+                    def _():
+                        add_to(1, ml, yrecv, ml)
+
+                    @pl.when(z < N_Z - 1)
+                    def _():
+                        left_copy(ml).wait_recv()
+                        part[1, ml] = (
+                            part[1, ml].astype(F32) + yrecv[ml].astype(F32) + zr[ml].astype(F32)
+                        ).astype(BF16)
+
+                left_copy(ml).start()
+
+        mz = s - Z_SUM_LAG
+
+        @pl.when((mz >= 0) & (mz < MESSAGES))
+        def _():
+            @pl.when(z_first(mz) & (z_of(mz) == z))
+            def _():
+                n = lax.rem(mz // PARTS, N_Z)
+
+                @pl.when(z == 0)
+                def _():
+                    left_other(mz).wait_recv()
+                    add_to(0, mz, zr2, n)
 
                 @pl.when(z == N_Z - 1)
                 def _():
-                    part[1, ml] = (part[1, ml].astype(F32) + yrecv[ml].astype(F32)).astype(BF16)
-
-                @pl.when(z < N_Z - 1)
-                def _():
-                    left_copy(ml).wait_recv()
-                    part[1, ml] = (
-                        part[1, ml].astype(F32) + yrecv[ml].astype(F32) + zr[ml].astype(F32)
+                    right_other(mz).wait_recv()
+                    add_to(0, mz, zl2, n)
+
+                @pl.when((z > 0) & (z < N_Z - 1))
+                def _():
+                    left_other(mz).wait_recv()
+                    right_other(mz).wait_recv()
+                    part[0, mz] = (
+                        part[0, mz].astype(F32) + zl2[n].astype(F32) + zr2[n].astype(F32)
                     ).astype(BF16)
 
-                left_copy(ml).start()
+                y_copy(mz).start()
 
         mf = s - FINAL_LAG
 
@@ -363,11 +447,19 @@
 
     @pl.loop(0, MESSAGES)
     def _(m):
-        y_copy(m).wait_send()
+        early = z_first(m)
+
+        @pl.when(jnp.logical_not(early) | (z_of(m) == z))
+        def _():
+            y_copy(m).wait_send()
 
         @pl.when(z_of(m) != z)
         def _():
             right_copy(m).wait_send()
+
+            @pl.when(early)
+            def _():
+                right_other(m).wait_send()
 
     @pl.loop(1, tensor)
     def _(k):
@@ -413,6 +505,8 @@
             pltpu.VMEM((MESSAGES, rows // PARTS, width), BF16),
             pltpu.VMEM((MESSAGES, rows // PARTS, width), BF16),
             pltpu.VMEM((MESSAGES, rows // PARTS, width), BF16),
+            pltpu.VMEM((N_Z, rows // PARTS, width), BF16),
+            pltpu.VMEM((N_Z, rows // PARTS, width), BF16),
             pltpu.VMEM((W_SLOTS, depth, width), BF16),
             pltpu.VMEM((2, 2, stage_rows, depth), BF16),
             pltpu.VMEM((adapters, rank, depth), BF16),
@@ -421,6 +515,7 @@
             pltpu.VMEM((N_Z, rows // 2, 2 * rank), BF16),
             pltpu.VMEM((rows, adapters * rank), BF16),
             dma((MESSAGES,)), dma((MESSAGES,)), dma((MESSAGES,)), dma((MESSAGES,)), dma((MESSAGES,)),
+            dma((N_Z,)), dma((N_Z,)), dma((N_Z,)),
             dma((W_SLOTS,)), dma((2, 2)),
             dma((tensor,)), dma((tensor,)), dma((tensor,)), dma((tensor,)),
             dma((tensor,)), dma((tensor,)), dma((tensor,)), dma((tensor,)),

time: 180 us -> 173 us (0.961)
  Pallas kernels: 176 us -> 169 us
    pallas_call x1, Pallas kernels: 176 us -> 169 us  [local_fused(): pl.pallas_call(fused, out_shape=jax.ShapeDtypeStruct((rows, block_cols),...]
where the time goes in v4:
time: 173 us
  Pallas kernels  169 us (98%)
  local copies, waits for them, and re-layouts  3.58 us (2%)
    pallas_call x1, Pallas kernels, local_fused(): pl.pallas_call(fused, out_shape=jax.ShapeDtypeStruct((rows, block_cols),...  169 us

profile of v4, /device:TPU:8, one launch (start us, length us, event | category | flops | bytes accessed | tf_op | source)
XLA Modules:
  0.0 172.9 jit_solution(18442483308094404311)
XLA Ops:
  0.0 0.8 select_reduce_fusion
  0.8 0.9 broadcast_in_dim.23.pos
  1.7 168.5 %shard_map.73 = bf16[768,1024]{1,0:T(8,128)(2,1)} custom-call(bf16[768,2048]{1,0:T(8,128)(2,1)} %gate.1, bf16[768,2048]{1,0:T(8,128)(2,1)} %up.1, bf16[2048,8192]{1,0:T(8,128)(2,1)} %w.1, bf16[1,64,16384]{2,1,0:T(8,128)(2,1)} %a.1, bf16[1,64,8192]{2,1,0:T(8,128)(2,1)} %b.1, s32[768,128]{1,0:T(8,128)} %broadcast_in_dim.23.pos), custom_call_target="tpu_custom_call" | custom-call | tf_op jit(solution)/shard_map/pallas_call | solution.py:497
  170.2 2.7 %copy.9 = bf16[768,1024]{1,0:T(8,128)(2,1)} copy(bf16[768,1024]{1,0:T(8,128)(2,1)} %shard_map.73) | data formatting | bytes 3145728

commit v5 on v4

--- a/solution.py
+++ b/solution.py
@@ -11,13 +11,13 @@
 F32, BF16 = jnp.float32, jnp.bfloat16
 N_Y, N_Z = 2, 4
 CHUNKS = 4
-PARTS = 2
+PARTS = 3
 MESSAGES = CHUNKS * N_Z * PARTS
 W_SLOTS = 4
-Y_LAG, HOP_LAG = 3, 2
+Y_LAG, HOP_LAG = 6, 3
 Z_FIRST = 1
 Z_SUM_LAG = Y_LAG + HOP_LAG * (N_Z - 1) + 2
-LOW_STEP, PAIR_STEP, SUM_STEP, FINAL_LAG = 18, 21, 24, 25
+LOW_STEP, PAIR_STEP, SUM_STEP, FINAL_LAG = 27, 31, 36, 37
 STEPS = MESSAGES + FINAL_LAG
 
 

time: 173 us -> 172 us (level)
  Pallas kernels: 169 us -> 167 us
where the time goes in v5:
time: 172 us; the launch traced here: 171 us
  Pallas kernels  167 us (97%)
  local copies, waits for them, and re-layouts  3.58 us (2%)
    pallas_call x1, Pallas kernels, local_fused(): pl.pallas_call(fused, out_shape=jax.ShapeDtypeStruct((rows, block_cols),...  167 us

profile of v5, /device:TPU:8, one launch (start us, length us, event | category | flops | bytes accessed | tf_op | source)
XLA Modules:
  0.0 171.4 jit_solution(8741084547721139267)
XLA Ops:
  0.0 0.8 select_reduce_fusion
  0.8 0.9 broadcast_in_dim.23.pos
  1.7 167.0 %shard_map.73 = bf16[768,1024]{1,0:T(8,128)(2,1)} custom-call(bf16[768,2048]{1,0:T(8,128)(2,1)} %gate.1, bf16[768,2048]{1,0:T(8,128)(2,1)} %up.1, bf16[2048,8192]{1,0:T(8,128)(2,1)} %w.1, bf16[1,64,16384]{2,1,0:T(8,128)(2,1)} %a.1, bf16[1,64,8192]{2,1,0:T(8,128)(2,1)} %b.1, s32[768,128]{1,0:T(8,128)} %broadcast_in_dim.23.pos), custom_call_target="tpu_custom_call" | custom-call | tf_op jit(solution)/shard_map/pallas_call | solution.py:497
  168.8 2.7 %copy.9 = bf16[768,1024]{1,0:T(8,128)(2,1)} copy(bf16[768,1024]{1,0:T(8,128)(2,1)} %shard_map.73) | data formatting | bytes 3145728
